TPU v7x, 32 devices: a whole 2x2x4 slice. The times are simulated.
32 devices in a mesh: row: 4 (over x, core), col: 8 (over z, y).
Axes of the slice: x: 2, y: 2, z: 4, core: 2. Of those that a mesh axis runs over, the one named last changes fastest.
Arguments:
- send_cells: int32 [32, 32, 512], P(('row', 'col')), may hold values from 0 to 65535, as said below
- send_species: int32 [32, 32, 512], P(('row', 'col')), may hold values from 0 to 5
- send_mix: bfloat16 [32, 6, 32, 512], P(('row', 'col')), may hold values from 0 to 0.5
- send_counts: int32 [32, 32], P(('row', 'col')), may hold values from 64 to 512, as said below
- chi: float32 [6, 6], replicated, may hold values from 0 to 8
Outputs:
- forces: float32 [32, 3, 32, 512], P(('row', 'col'))
Inputs may be any that keep to these rules, and one draw needn't show every extreme that they name: `send_cells`: local cell (x * 16 + y) * 256 + z in the destination brick; domain s (flat index) holds particles with z from s * 8 to (s + 1) * 8 - 1 only. `send_counts`: slots at or beyond the count are unused. At most 512 particles go from one domain to one brick; in every draw some domain fills a slot list, and one brick receives 512 from every domain.
All inputs are finite; a program needn't handle non-finite values.
Results may differ from a plain program's by a relative error of at most 0.0023.
Values may be sent and summed in bfloat16 or wider, within the bound.
A program may use at most 256 MiB of HBM per device.

v0:
```python
import jax
import jax.numpy as jnp
from jax import lax
from jax.sharding import PartitionSpec as P

SPECIES = 6
BX = 16
BY = 16
NZ = 256


raw_taps = (0.1353352832366127, 0.6065306597126334, 1.0, 0.6065306597126334, 0.1353352832366127)
tap_total = sum(raw_taps)
taps = tuple((t / tap_total for t in raw_taps))
rho_ref = 2.0
inv_kappa = 1.0


def extended_2(value, sides, width):
    for axis, dim in sides:
        count, length = (lax.axis_size(axis), value.shape[dim])
        up = [(i, (i + 1) % count) for i in range(count)]
        down = [(j, i) for i, j in up]
        last = lax.slice_in_dim(value, length - width, length, axis=dim)
        first = lax.slice_in_dim(value, 0, width, axis=dim)
        before = lax.ppermute(last, axis, up)
        after = lax.ppermute(first, axis, down)
        value = jnp.concatenate([before, value, after], axis=dim)
    return value


def smooth(padded):
    width_x = padded.shape[1] - 4
    width_y = padded.shape[2] - 4
    along_x = taps[0] * padded[:, 0:width_x]
    for t in range(1, 5):
        along_x = along_x + taps[t] * padded[:, t : t + width_x]
    along_y = taps[0] * along_x[:, :, 0:width_y]
    for t in range(1, 5):
        along_y = along_y + taps[t] * along_x[:, :, t : t + width_y]
    along_z = taps[0] * jnp.roll(along_y, 2, axis=3)
    for t in range(1, 5):
        along_z = along_z + taps[t] * jnp.roll(along_y, 2 - t, axis=3)
    return along_z


def potential_of(filtered, chi):
    count = chi.shape[0]
    chis = 0.5 * (chi + chi.T) * (1.0 - jnp.eye(count, dtype=jnp.float32))
    mixing = jnp.einsum("kl,lxyz->kxyz", chis, filtered, precision=lax.Precision.HIGHEST) / rho_ref
    total = jnp.sum(filtered, axis=0) / rho_ref
    return mixing + inv_kappa * (total[None] - 1.0)


def deposit(weights, plane_idx, z_offset, plane, band, blocks):
    sources = plane_idx.shape[0]
    rows = plane_idx.shape[1]
    per = sources // blocks
    w_blocks = jnp.moveaxis(weights.reshape(SPECIES, blocks, per, rows), 1, 0)
    i_blocks = plane_idx.reshape(blocks, per, rows)
    z_blocks = z_offset.reshape(blocks, per, rows)
    plane_ids = jnp.arange(plane, dtype=jnp.int32)
    band_ids = jnp.arange(band, dtype=jnp.int32)

    def deposit_one_block(carry, item):
        w_b, i_b, z_b = item
        table = (i_b[:, :, None] == plane_ids[None, None, :]).astype(jnp.bfloat16)
        banded = jnp.where(
            z_b[None, :, :, None] == band_ids[None, None, None, :],
            w_b[:, :, :, None],
            jnp.zeros((), jnp.bfloat16),
        )
        return (
            carry,
            jnp.einsum("kbpz,bpc->bkzc", banded, table, preferred_element_type=jnp.float32),
        )

    unused, tiles = lax.scan(deposit_one_block, 0, (w_blocks, i_blocks, z_blocks))
    tiles = tiles.reshape(sources, SPECIES, band, plane)
    return jnp.transpose(tiles, (1, 3, 0, 2)).reshape(SPECIES, plane, sources * band)


def pick_forces(grads, plane_idx, z_offset, weights_f, blocks):
    sources = plane_idx.shape[0]
    rows = plane_idx.shape[1]
    plane = grads.shape[2]
    band = grads.shape[3] // sources
    per = sources // blocks
    tiles = jnp.transpose(grads.reshape(3 * SPECIES, plane, sources, band), (2, 0, 3, 1))
    g_blocks = tiles.reshape(blocks, per, 3 * SPECIES, band, plane)
    i_blocks = plane_idx.reshape(blocks, per, rows)
    z_blocks = z_offset.reshape(blocks, per, rows)
    w_blocks = jnp.moveaxis(weights_f.reshape(SPECIES, blocks, per, rows), 0, 2)
    plane_ids = jnp.arange(plane, dtype=jnp.int32)
    band_ids = jnp.arange(band, dtype=jnp.int32)

    def pick_one_block(carry, item):
        g_b, i_b, z_b, w_b = item
        table = (i_b[:, :, None] == plane_ids[None, None, :]).astype(jnp.float32)
        values = jnp.einsum("bjzc,bpc->bjzp", g_b, table, precision=lax.Precision.HIGHEST)
        chosen = jnp.sum(
            jnp.where(z_b[:, None, None, :] == band_ids[None, None, :, None], values, 0.0), axis=2
        )
        chosen = chosen.reshape(per, 3, SPECIES, rows)
        return (carry, -jnp.sum(w_b[:, None] * chosen, axis=2))

    unused, result = lax.scan(pick_one_block, 0, (g_blocks, i_blocks, z_blocks, w_blocks))
    return jnp.transpose(result.reshape(sources, 3, rows), (1, 0, 2))


def body(send_cells, send_species, send_mix, send_counts, chi):
    species = send_species[0]
    mixture = send_mix[0]
    counts = send_counts[0]
    domains = mixture.shape[1]
    slots = mixture.shape[2]
    band = NZ // domains
    valid = jnp.arange(slots, dtype=jnp.int32)[None, :] < counts[:, None]
    onehot = (species[None] == jnp.arange(SPECIES, dtype=jnp.int32)[:, None, None]).astype(
        jnp.float32
    )
    weights = jnp.where(valid[None], onehot + mixture.astype(jnp.float32), 0.0).astype(jnp.bfloat16)
    got_weights, got_cells = (
        lax.all_to_all(weights, ("row", "col"), split_axis=1, concat_axis=1, tiled=True),
        lax.all_to_all(send_cells, ("row", "col"), split_axis=1, concat_axis=1, tiled=True),
    )
    place = got_cells.reshape(domains, slots)
    density = deposit(
        got_weights, place // NZ, place % NZ % band, BX * BY, band, max(1, domains // 8)
    )
    density = density.reshape(SPECIES, BX, BY, NZ)
    flat_w = got_weights.astype(jnp.float32)
    padded = extended_2(density, (("row", 1), ("col", 2)), 2)
    potential = potential_of(smooth(padded), chi)
    extended = extended_2(potential, (("row", 1), ("col", 2)), 1)
    center = extended[:, 1:-1, 1:-1]
    grad_x = 0.5 * (extended[:, 2:, 1:-1] - extended[:, :-2, 1:-1])
    grad_y = 0.5 * (extended[:, 1:-1, 2:] - extended[:, 1:-1, :-2])
    grad_z = 0.5 * (jnp.roll(center, -1, axis=3) - jnp.roll(center, 1, axis=3))
    grads = jnp.stack((grad_x, grad_y, grad_z), axis=0).reshape(3, SPECIES, BX * BY, NZ)
    slot_forces = pick_forces(grads, place // NZ, place % NZ % band, flat_w, max(1, domains // 8))
    returned = lax.all_to_all(slot_forces, ("row", "col"), split_axis=1, concat_axis=1, tiled=True)
    return returned[None]


def solution(mesh):
    return jax.shard_map(
        body,
        mesh=mesh,
        in_specs=(
            P(("row", "col"), None, None),
            P(("row", "col"), None, None),
            P(("row", "col"), None, None, None),
            P(("row", "col"), None),
            P(),
        ),
        out_specs=P(("row", "col"), None, None, None),
        check_vma=False,
    )
```

profile of v0, /device:TPU:0, one launch (start us, length us, event | category | flops | bytes accessed | tf_op | source)
XLA Modules:
  0.0 197.6 jit_solution(6065675632477298162)
XLA Ops:
  0.0 1.5 copy.82
  1.5 7.3 %all-to-all-start.1 = ((s32[1,32,512]{2,0,1:T(1,128)}), s32[1,32,512]{2,0,1:T(1,128)S(1)}, u32[]{:S(2)}, u32[]{:S(2)}) async-start(s32[1,32,512]{2,0,1:T(1,128)} %copy.82), calls=%async_computation.1 | async-start | bytes 131072 | tf_op jit(solution)/shard_map/all_to_all | solution.py:125
  9.6 1.8 fusion.53
  11.4 4.7 %all-to-all-done.1 = s32[1,32,512]{2,0,1:T(1,128)S(1)} async-done(((s32[1,32,512]{2,0,1:T(1,128)}), s32[1,32,512]{2,0,1:T(1,128)S(1)}, u32[]{:S(2)}, u32[]{:S(2)}) %all-to-all-start.1) | async-done | bytes 65568 | tf_op jit(solution)/shard_map/all_to_all | solution.py:125
  16.1 2.6 %all-to-all-start = ((bf16[6,32,512]{2,0,1:T(8,128)(2,1)}), bf16[6,32,512]{2,0,1:T(8,128)(2,1)S(1)}, u32[]{:S(2)}, u32[]{:S(2)}) async-start(bf16[6,32,512]{2,0,1:T(8,128)(2,1)} %fusion.53), calls=%async_computation | async-start | bytes 524288 | tf_op jit(solution)/shard_map/all_to_all | solution.py:124
  18.8 10.5 %all-to-all-done = bf16[6,32,512]{2,0,1:T(8,128)(2,1)S(1)} async-done(((bf16[6,32,512]{2,0,1:T(8,128)(2,1)}), bf16[6,32,512]{2,0,1:T(8,128)(2,1)S(1)}, u32[]{:S(2)}, u32[]{:S(2)}) %all-to-all-start) | async-done | bytes 196640 | tf_op jit(solution)/shard_map/all_to_all | solution.py:124
  29.4 9.6 %while.22 = (s32[]{:T(128)}, f32[4,8,6,8,256]{4,3,2,1,0:T(8,128)S(1)}, s32[4,8,512]{2,1,0:T(8,128)S(1)}, bf16[4,6,8,512]{3,1,2,0:T(8,128)(2,1)S(1)}, s32[4,8,512]{2,1,0:T(8,128)S(1)}, /*index=5*/s32[]{:T(128)}) while((s32[]{:T(128)}, f32[4,8,6,8,256]{4,3,2,1,0:T(8,128)S(1)}, s32[4,8,512]{2,1,0:T(8,128)S(1)}, ...), condition=%wide.region_1.2_spmd.clone, body=%wide.region_0.1_spmd.clone.sunk | while | flops 101941248 | bytes 720977 | solution.py:78
  29.4 2.3 %fusion.84 = f32[4,8,6,8,256]{4,3,2,1,0:T(8,128)S(1)} fusion(f32[4,8,6,8,256]{4,3,2,1,0:T(8,128)S(1)} %get-tuple-element.304, s32[]{:T(128)} %get-tuple-element.303, s32[8,512]{1,0:T(8,128)S(1)} %get-tuple-element.287, pred[8,512,8]{1,2,0:T(8,128)(4,1)S(1)} %iota_compare_fusion.10, bf16[6,8,512]{2,0,1:T(8,128)(2,1)S(1)} %dynamic-slice_bitcast_fusion.11), kind=kOutput, calls=%fused_computation.9.clone.1 | convolution fusion | flops 101908480 | bytes 507908 | tf_op jit(solution)/shard_map/while/body/eval_jaxpr/kbpz,bpc->bkzc/dot_general | solution.py:75
  31.8 2.3 %fusion.84 = f32[4,8,6,8,256]{4,3,2,1,0:T(8,128)S(1)} fusion(f32[4,8,6,8,256]{4,3,2,1,0:T(8,128)S(1)} %get-tuple-element.304, s32[]{:T(128)} %get-tuple-element.303, s32[8,512]{1,0:T(8,128)S(1)} %get-tuple-element.287, pred[8,512,8]{1,2,0:T(8,128)(4,1)S(1)} %iota_compare_fusion.10, bf16[6,8,512]{2,0,1:T(8,128)(2,1)S(1)} %dynamic-slice_bitcast_fusion.11), kind=kOutput, calls=%fused_computation.9.clone.1 | convolution fusion | flops 101908480 | bytes 507908 | tf_op jit(solution)/shard_map/while/body/eval_jaxpr/kbpz,bpc->bkzc/dot_general | solution.py:75
  34.2 2.3 %fusion.84 = f32[4,8,6,8,256]{4,3,2,1,0:T(8,128)S(1)} fusion(f32[4,8,6,8,256]{4,3,2,1,0:T(8,128)S(1)} %get-tuple-element.304, s32[]{:T(128)} %get-tuple-element.303, s32[8,512]{1,0:T(8,128)S(1)} %get-tuple-element.287, pred[8,512,8]{1,2,0:T(8,128)(4,1)S(1)} %iota_compare_fusion.10, bf16[6,8,512]{2,0,1:T(8,128)(2,1)S(1)} %dynamic-slice_bitcast_fusion.11), kind=kOutput, calls=%fused_computation.9.clone.1 | convolution fusion | flops 101908480 | bytes 507908 | tf_op jit(solution)/shard_map/while/body/eval_jaxpr/kbpz,bpc->bkzc/dot_general | solution.py:75
  36.6 2.3 %fusion.84 = f32[4,8,6,8,256]{4,3,2,1,0:T(8,128)S(1)} fusion(f32[4,8,6,8,256]{4,3,2,1,0:T(8,128)S(1)} %get-tuple-element.304, s32[]{:T(128)} %get-tuple-element.303, s32[8,512]{1,0:T(8,128)S(1)} %get-tuple-element.287, pred[8,512,8]{1,2,0:T(8,128)(4,1)S(1)} %iota_compare_fusion.10, bf16[6,8,512]{2,0,1:T(8,128)(2,1)S(1)} %dynamic-slice_bitcast_fusion.11), kind=kOutput, calls=%fused_computation.9.clone.1 | convolution fusion | flops 101908480 | bytes 507908 | tf_op jit(solution)/shard_map/while/body/eval_jaxpr/kbpz,bpc->bkzc/dot_general | solution.py:75
  39.1 6.7 %reshape_reshape.6 = f32[6,16,16,256]{2,1,3,0:T(8,128)} reshape(f32[6,256,32,8]{1,3,2,0:T(8,128)S(1)} %copy_bitcast_fusion.2) | data formatting | bytes 3145728 | tf_op jit(solution)/shard_map/reshape;reshape | solution.py:131
  45.7 5.9 %fusion.70 = (f32[6,2,16,256]{2,1,3,0:T(2,128)S(1)}, f32[6,2,16,256]{2,1,3,0:T(2,128)S(1)}) fusion(f32[6,16,16,256]{2,1,3,0:T(8,128)} %reshape_reshape.6), kind=kLoop, calls=%fused_computation.121 | loop fusion | bytes 786432 | tf_op jit(solution)/shard_map/slice | solution.py:24
  51.6 1.7 copy.86
  53.9 1.8 collective-permute-start.1
  55.7 8.9 %copy.88 = f32[6,16,16,256]{3,2,1,0:T(8,128)S(1)} copy(f32[6,16,16,256]{2,1,3,0:T(8,128)} %reshape_reshape.6) | data formatting | bytes 3145728 | tf_op jit(solution)/shard_map/reshape;reshape | solution.py:131
  64.8 1.1 collective-permute-start.2
  65.9 3.7 %collective-permute-start.3 = (f32[6,20,2,256]{3,2,1,0:T(2,128)S(1)}, f32[6,20,2,256]{3,2,1,0:T(2,128)S(1)}, u32[]{:S(2)}, u32[]{:S(2)}) collective-permute-start(f32[6,20,2,256]{3,2,1,0:T(2,128)S(1)} %get-tuple-element.210), channel_id=1, source_target_pairs={{1,0},{2,1},{3,2},{4,3},{5,4},{6,5},{7,6},{0,7},{9,8},{10,9},{11,1... | collective-permute-start | bytes 737288 | tf_op jit(solution)/shard_map/ppermute | solution.py:27
  70.5 4.9 %collective-permute-done.2 = f32[6,20,2,256]{3,2,1,0:T(2,128)S(1)} collective-permute-done((f32[6,20,2,256]{3,2,1,0:T(2,128)S(1)}, f32[6,20,2,256]{3,2,1,0:T(2,128)S(1)}, u32[]{:S(2)}, u32[]{:S(2)}) %collective-permute-start.2) | collective-permute-done | bytes 245792 | tf_op jit(solution)/shard_map/ppermute | solution.py:26
  75.4 2.2 %collective-permute-done.3 = f32[6,20,2,256]{3,2,1,0:T(2,128)S(1)} collective-permute-done((f32[6,20,2,256]{3,2,1,0:T(2,128)S(1)}, f32[6,20,2,256]{3,2,1,0:T(2,128)S(1)}, u32[]{:S(2)}, u32[]{:S(2)}) %collective-permute-start.3) | collective-permute-done | bytes 245792 | tf_op jit(solution)/shard_map/ppermute | solution.py:27
  78.7 0.9 fusion.44
  81.3 2.2 %fusion.68 = (f32[16,16,256]{2,1,0:T(8,128)S(1)}, f32[6,16,16,256]{3,2,1,0:T(8,128)S(1)}) fusion(f32[6,16,16,2]{3,2,1,0:T(8,128)S(1)} %get-tuple-element.212, f32[6,16,16,254]{3,2,1,0:T(8,128)S(1)} %get-tuple-element.214, f32[6,16,16,1]{3,2,1,0:T(8,128)S(1)} %get-tuple-element.216, f32[6,16,16,255]{3,2,1,0:T(8,128)S(1)} %get-tuple-element.218, ...), kind=kLoop, calls=%fused_computation.120 | loop fusion | flops 8978432 | bytes 15990784 | tf_op jit(solution)/shard_map/reduce_sum | solution.py:51
  83.5 2.9 %multiply_add_fusion = f32[6,16,16,256]{3,0,2,1:T(8,128)S(1)} fusion(f32[6,16,16,256]{3,2,1,0:T(8,128)S(1)} %get-tuple-element.192, f32[16,16,256]{2,1,0:T(8,128)S(1)} %multiply_add_fusion.1, f32[6,6]{1,0:T(8,128)S(1)} %copy-done.3, f32[6,6]{0,1:T(8,128)S(1)} %copy.83), kind=kOutput, calls=%fused_computation.63 | convolution fusion | flops 29098200 | bytes 3408160 | tf_op jit(solution)/shard_map/kl,lxyz->kxyz/dot_general | solution.py:50
  87.1 2.7 %slice_bitcast_fusion = (f32[1,6,16,16,255]{4,1,3,2,0:T(8,128)}, f32[1,6,16,16,255]{4,1,3,2,0:T(8,128)}) fusion(f32[6,16,16,256]{3,0,2,1:T(8,128)S(1)} %multiply_add_fusion), kind=kLoop, calls=%fused_computation.43 | loop fusion | bytes 6266880 | tf_op jit(solution)/shard_map/jit(_roll_static)/concatenate | solution.py:139
  90.3 1.4 fusion.72
  91.7 2.5 %copy.92 = f32[6,16,16,1]{2,1,0,3:T(8,128)} copy(f32[6,16,16,1]{3,0,2,1:T(8,128)} %get-tuple-element.206) | data formatting | bytes 12288 | tf_op jit(solution)/shard_map/jit(_roll_static)/slice | solution.py:139
  94.1 2.4 %copy.93 = f32[1,6,16,16,1]{4,1,3,2,0:T(8,128)} copy(f32[1,6,16,16,1]{3,2,1,4,0:T(8,128)} %bitcast.147) | data formatting | bytes 12288 | tf_op jit(solution)/shard_map/jit(_roll_static)/concatenate | solution.py:139
  96.6 1.3 copy.94
  97.8 2.5 %copy.95 = f32[1,6,16,16,1]{4,1,3,2,0:T(8,128)} copy(f32[1,6,16,16,1]{3,2,1,4,0:T(8,128)} %bitcast.148) | data formatting | bytes 12288 | tf_op jit(solution)/shard_map/jit(_roll_static)/concatenate | solution.py:139
  100.4 1.2 collective-permute-start.6
  101.6 0.9 collective-permute-start.7
  102.5 2.8 %fusion.39 = f32[1,6,16,16,256]{4,1,3,2,0:T(8,128)S(1)} fusion(f32[1,6,16,16,1]{4,1,3,2,0:T(8,128)S(1)} %copy-done.1, f32[1,6,16,16,255]{4,1,3,2,0:T(8,128)} %get-tuple-element.208, f32[1,6,16,16,255]{4,1,3,2,0:T(8,128)S(1)} %copy-done, f32[1,6,16,16,1]{4,1,3,2,0:T(8,128)} %copy.95), kind=kLoop, calls=%fused_computation.60 | loop fusion | flops 1572864 | bytes 4718592 | tf_op jit(solution)/shard_map/mul | solution.py:139
  105.3 1.8 collective-permute-done.6
  107.0 3.9 %collective-permute-done.7 = f32[6,18,1,256]{3,0,2,1:T(8,128)S(1)} collective-permute-done((f32[6,18,1,256]{3,0,2,1:T(8,128)S(1)}, f32[6,18,1,256]{3,0,2,1:T(8,128)S(1)}, u32[]{:S(2)}, u32[]{:S(2)}) %collective-permute-start.7) | collective-permute-done | bytes 110624 | tf_op jit(solution)/shard_map/ppermute | solution.py:26
  110.9 1.0 fusion.38
  112.0 3.4 %pad_maximum_fusion = f32[3,6,16,16,256]{4,1,3,2,0:T(8,128)} fusion(f32[1,6,16,16,256]{4,1,3,2,0:T(8,128)S(1)} %fusion.39, f32[1,6,16,16,256]{4,1,3,2,0:T(8,128)S(1)} %get-tuple-element.200, f32[1,6,16,16,256]{4,1,3,2,0:T(8,128)S(1)} %get-tuple-element.199), kind=kLoop, calls=%fused_computation.32 | loop fusion | flops 2359296 | bytes 9437184 | tf_op jit(solution)/shard_map/stack | solution.py:140
  115.4 18.7 %copy.96 = f32[3,6,16,16,256]{3,2,4,1,0:T(8,128)} copy(f32[3,6,16,16,256]{4,1,3,2,0:T(8,128)} %pad_maximum_fusion) | data formatting | bytes 9437184 | tf_op jit(solution)/shard_map/stack | solution.py:140
  134.1 26.4 %reshape_reshape.7 = f32[18,256,32,8]{1,3,2,0:T(8,128)} reshape(f32[3,6,16,16,256]{3,2,4,1,0:T(8,128)} %copy.96) | data formatting | bytes 9437184 | tf_op jit(solution)/shard_map/reshape;reshape | solution.py:89
  160.5 22.5 %while.23 = (s32[]{:T(128)}, f32[4,8,3,512]{3,1,2,0:T(8,128)S(1)}, f32[4,8,6,512]{3,1,0,2:T(8,128)}, s32[4,8,512]{2,1,0:T(8,128)S(1)}, f32[4,8,18,8,256]{4,3,1,0...) while((s32[]{:T(128)}, f32[4,8,3,512]{3,1,2,0:T(8,128)S(1)}, f32[4,8,6,512]{3,1,0,2:T(8,128)}, ...), condition=%wide.region_6.7_spmd.clone, body=%wide.region_3.6_spmd.clone.sunk | while | flops 1814274048 | bytes 2966105 | solution.py:107
  160.5 4.4 %select_reduce_fusion.2 = f32[8,18,512]{2,1,0:T(8,128)S(1)} fusion(s32[8,512]{1,0:T(8,128)S(1)} %get-tuple-element.295, pred[8,8,512]{2,1,0:T(8,128)(4,1)S(1)} %iota_compare_fusion.11, f32[4,8,18,8,256]{4,3,1,0,2:T(8,128)} %get-tuple-element.333, s32[]{:T(128)} %get-tuple-element.322), kind=kOutput, calls=%fused_computation.22.clone.1 | convolution fusion | flops 1814093824 | bytes 1524224 | tf_op jit(solution)/shard_map/while/body/eval_jaxpr/bjzc,bpc->bjzp/dot_general | solution.py:100
  165.1 0.9 dynamic-slice_bitcast_fusion.13
  166.2 4.4 %select_reduce_fusion.2 = f32[8,18,512]{2,1,0:T(8,128)S(1)} fusion(s32[8,512]{1,0:T(8,128)S(1)} %get-tuple-element.295, pred[8,8,512]{2,1,0:T(8,128)(4,1)S(1)} %iota_compare_fusion.11, f32[4,8,18,8,256]{4,3,1,0,2:T(8,128)} %get-tuple-element.333, s32[]{:T(128)} %get-tuple-element.322), kind=kOutput, calls=%fused_computation.22.clone.1 | convolution fusion | flops 1814093824 | bytes 1524224 | tf_op jit(solution)/shard_map/while/body/eval_jaxpr/bjzc,bpc->bjzp/dot_general | solution.py:100
  170.8 0.9 dynamic-slice_bitcast_fusion.13
  171.8 4.4 %select_reduce_fusion.2 = f32[8,18,512]{2,1,0:T(8,128)S(1)} fusion(s32[8,512]{1,0:T(8,128)S(1)} %get-tuple-element.295, pred[8,8,512]{2,1,0:T(8,128)(4,1)S(1)} %iota_compare_fusion.11, f32[4,8,18,8,256]{4,3,1,0,2:T(8,128)} %get-tuple-element.333, s32[]{:T(128)} %get-tuple-element.322), kind=kOutput, calls=%fused_computation.22.clone.1 | convolution fusion | flops 1814093824 | bytes 1524224 | tf_op jit(solution)/shard_map/while/body/eval_jaxpr/bjzc,bpc->bjzp/dot_general | solution.py:100
  176.4 0.9 dynamic-slice_bitcast_fusion.13
  177.4 4.4 %select_reduce_fusion.2 = f32[8,18,512]{2,1,0:T(8,128)S(1)} fusion(s32[8,512]{1,0:T(8,128)S(1)} %get-tuple-element.295, pred[8,8,512]{2,1,0:T(8,128)(4,1)S(1)} %iota_compare_fusion.11, f32[4,8,18,8,256]{4,3,1,0,2:T(8,128)} %get-tuple-element.333, s32[]{:T(128)} %get-tuple-element.322), kind=kOutput, calls=%fused_computation.22.clone.1 | convolution fusion | flops 1814093824 | bytes 1524224 | tf_op jit(solution)/shard_map/while/body/eval_jaxpr/bjzc,bpc->bjzp/dot_general | solution.py:100
  182.0 0.9 dynamic-slice_bitcast_fusion.13
  183.1 13.8 %all_to_all.15 = f32[3,32,512]{2,0,1:T(4,128)S(1)} all-to-all(f32[3,32,512]{2,0,1:T(4,128)S(1)} %bitcast.145), channel_id=1, replica_groups=mesh['row'=4,'col'=8] {'row','col'}, dimensions={1} | all-to-all | bytes 393216 | tf_op jit(solution)/shard_map/all_to_all | solution.py:142
  (67 shorter events, 8.8 us)
Async XLA Ops:
  1.5 14.6 %all-to-all-start.1 = ((s32[1,32,512]{2,0,1:T(1,128)}), s32[1,32,512]{2,0,1:T(1,128)S(1)}, u32[]{:S(2)}, u32[]{:S(2)}) async-start(s32[1,32,512]{2,0,1:T(1,128)} %copy.82), calls=%async_computation.1 | async-start | bytes 131072 | tf_op jit(solution)/shard_map/all_to_all | solution.py:125
  16.1 13.2 %all-to-all-start = ((bf16[6,32,512]{2,0,1:T(8,128)(2,1)}), bf16[6,32,512]{2,0,1:T(8,128)(2,1)S(1)}, u32[]{:S(2)}, u32[]{:S(2)}) async-start(bf16[6,32,512]{2,0,1:T(8,128)(2,1)} %fusion.53), calls=%async_computation | async-start | bytes 524288 | tf_op jit(solution)/shard_map/all_to_all | solution.py:124
  53.3 11.3 %collective-permute-start = (f32[6,2,16,256]{3,2,1,0:T(8,128)}, f32[6,2,16,256]{3,2,1,0:T(8,128)S(1)}, u32[]{:S(2)}, u32[]{:S(2)}) collective-permute-start(f32[6,2,16,256]{3,2,1,0:T(8,128)} %copy.86), channel_id=1, source_target_pairs={{0,8},{8,16},{16,24},{24,0},{1,9},{9,17},{17,25},{25,1},{2,10},{10... | collective-permute-start | bytes 589832 | tf_op jit(solution)/shard_map/ppermute | solution.py:26
  53.9 10.7 %collective-permute-start.1 = (f32[6,2,16,256]{3,2,1,0:T(8,128)S(1)}, f32[6,2,16,256]{3,2,1,0:T(8,128)S(1)}, u32[]{:S(2)}, u32[]{:S(2)}) collective-permute-start(f32[6,2,16,256]{3,2,1,0:T(8,128)S(1)} %copy.87), channel_id=1, source_target_pairs={{8,0},{16,8},{24,16},{0,24},{9,1},{17,9},{25,17},{1,25},{10,2},{18... | collective-permute-start | bytes 589832 | tf_op jit(solution)/shard_map/ppermute | solution.py:27
  64.6 5.0 %copy-start.3 = (f32[6,6]{1,0:T(8,128)S(1)}, f32[6,6]{1,0:T(8,128)}, u32[]{:S(2)}) copy-start(f32[6,6]{1,0:T(8,128)} %param.13) | copy-start | bytes 436
  64.8 10.6 %collective-permute-start.2 = (f32[6,20,2,256]{3,2,1,0:T(2,128)S(1)}, f32[6,20,2,256]{3,2,1,0:T(2,128)S(1)}, u32[]{:S(2)}, u32[]{:S(2)}) collective-permute-start(f32[6,20,2,256]{3,2,1,0:T(2,128)S(1)} %get-tuple-element.209), channel_id=1, source_target_pairs={{0,1},{1,2},{2,3},{3,4},{4,5},{5,6},{6,7},{7,0},{8,9},{9,10},{10,1... | collective-permute-start | bytes 737288 | tf_op jit(solution)/shard_map/ppermute | solution.py:26
  65.9 11.8 %collective-permute-start.3 = (f32[6,20,2,256]{3,2,1,0:T(2,128)S(1)}, f32[6,20,2,256]{3,2,1,0:T(2,128)S(1)}, u32[]{:S(2)}, u32[]{:S(2)}) collective-permute-start(f32[6,20,2,256]{3,2,1,0:T(2,128)S(1)} %get-tuple-element.210), channel_id=1, source_target_pairs={{1,0},{2,1},{3,2},{4,3},{5,4},{6,5},{7,6},{0,7},{9,8},{10,9},{11,1... | collective-permute-start | bytes 737288 | tf_op jit(solution)/shard_map/ppermute | solution.py:27
  89.8 10.6 %collective-permute-start.4 = (f32[6,1,16,256]{3,0,2,1:T(8,128)}, f32[6,1,16,256]{3,0,2,1:T(8,128)S(1)}, u32[]{:S(2)}, u32[]{:S(2)}) collective-permute-start(f32[6,1,16,256]{3,0,2,1:T(8,128)} %get-tuple-element.204), channel_id=1, source_target_pairs={{8,0},{16,8},{24,16},{0,24},{9,1},{17,9},{25,17},{1,25},{10,2},{18... | collective-permute-start | bytes 294920 | tf_op jit(solution)/shard_map/ppermute | solution.py:27
  89.8 10.6 %collective-permute-start.5 = (f32[6,1,16,256]{3,0,2,1:T(8,128)}, f32[6,1,16,256]{3,0,2,1:T(8,128)S(1)}, u32[]{:S(2)}, u32[]{:S(2)}) collective-permute-start(f32[6,1,16,256]{3,0,2,1:T(8,128)} %get-tuple-element.203), channel_id=1, source_target_pairs={{0,8},{8,16},{16,24},{24,0},{1,9},{9,17},{17,25},{25,1},{2,10},{10... | collective-permute-start | bytes 294920 | tf_op jit(solution)/shard_map/ppermute | solution.py:26
  97.8 4.6 %copy-start.1 = (f32[1,6,16,16,1]{4,1,3,2,0:T(8,128)S(1)}, f32[1,6,16,16,1]{4,1,3,2,0:T(8,128)}, u32[]{:S(2)}) copy-start(f32[1,6,16,16,1]{4,1,3,2,0:T(8,128)} %copy.93) | copy-start | bytes 18436
  100.3 2.1 %copy-start = (f32[1,6,16,16,255]{4,1,3,2,0:T(8,128)S(1)}, f32[1,6,16,16,255]{4,1,3,2,0:T(8,128)}, u32[]{:S(2)}) copy-start(f32[1,6,16,16,255]{4,1,3,2,0:T(8,128)} %get-tuple-element.207) | copy-start | bytes 4700164
  100.4 6.7 %collective-permute-start.6 = (f32[6,18,1,256]{3,0,2,1:T(8,128)S(1)}, f32[6,18,1,256]{3,0,2,1:T(8,128)S(1)}, u32[]{:S(2)}, u32[]{:S(2)}) collective-permute-start(f32[6,18,1,256]{3,0,2,1:T(8,128)S(1)} %get-tuple-element.201), channel_id=1, source_target_pairs={{1,0},{2,1},{3,2},{4,3},{5,4},{6,5},{7,6},{0,7},{9,8},{10,9},{11,1... | collective-permute-start | bytes 331784 | tf_op jit(solution)/shard_map/ppermute | solution.py:27
  101.6 9.3 %collective-permute-start.7 = (f32[6,18,1,256]{3,0,2,1:T(8,128)S(1)}, f32[6,18,1,256]{3,0,2,1:T(8,128)S(1)}, u32[]{:S(2)}, u32[]{:S(2)}) collective-permute-start(f32[6,18,1,256]{3,0,2,1:T(8,128)S(1)} %get-tuple-element.202), channel_id=1, source_target_pairs={{0,1},{1,2},{2,3},{3,4},{4,5},{5,6},{6,7},{7,0},{8,9},{9,10},{10,1... | collective-permute-start | bytes 331784 | tf_op jit(solution)/shard_map/ppermute | solution.py:26
  134.1 26.4 %copy-start.2 = (f32[4,8,3,512]{3,1,2,0:T(8,128)S(1)}, f32[4,8,3,512]{3,1,2,0:T(8,128)}, u32[]{:S(2)}) copy-start(f32[4,8,3,512]{3,1,2,0:T(8,128)} %custom-call.1) | copy-start | bytes 589828
where the time goes:
time: 199 us; the launch traced here: 198 us
  local copies, waits for them, and re-layouts  91 us (46%)
  matrix products  29.8 us (15%)
  waiting for transfers between devices  28 us (14%)
  starting transfers between devices  19 us (10%)
  other arithmetic  15.4 us (8%)
  blocking collectives  13.8 us (7%)
    another operation x1, local copies, waits for them, and re-layouts, pick_forces(): grads.reshape(3 * SPECIES, plane, sources, band)  26.4 us
    another operation x1, local copies, waits for them, and re-layouts, body(): jnp.stack((grad_x, grad_y, grad_z), axis=0).reshape(3, SPECIES, BX * BY, NZ)  18.7 us
    dot_general x4, matrix products, pick_one_block(): jnp.einsum('bjzc,bpc->bjzp', g_b, table, precision=lax.Precision.HIGHEST)  17.7 us
    another operation x2, local copies, waits for them, and re-layouts, body(): density = density.reshape(SPECIES, BX, BY, NZ)  15.5 us
    all_to_all x1, blocking collectives, body(): lax.all_to_all(slot_forces, ('row', 'col'), split_axis=1, concat_axis=1,...  13.8 us
    all_to_all x1, waiting for transfers between devices, body(): lax.all_to_all(weights, ('row', 'col'), split_axis=1, concat_axis=1, tile...  10.5 us
    dot_general x4, matrix products, deposit_one_block(): jnp.einsum('kbpz,bpc->bkzc', banded, table, preferred_element_type=jnp.fl...  9.25 us
    ppermute x4, waiting for transfers between devices, extended_2(): before = lax.ppermute(last, axis, up)  8.83 us
  transfers between devices with their start and end apart: 10, of which 6 were waited for; matrix products, arithmetic and copies ran while one was open for 13% of the time, Pallas kernels for 0%

commit v1 on v0

v1 whole, which is shorter than its diff:
```python
import functools

import jax
import jax.numpy as jnp
import numpy as np
from jax import lax
from jax.experimental import pallas as pl
from jax.experimental.pallas import tpu as pltpu
from jax.sharding import PartitionSpec as P

BX = 16
BY = 16
NZ = 256
LANES = 128
HALF = LANES // BY
REACH = 3

raw_taps = (0.1353352832366127, 0.6065306597126334, 1.0, 0.6065306597126334, 0.1353352832366127)
tap_total = sum(raw_taps)
taps = tuple(t / tap_total for t in raw_taps)
rho_ref = 2.0
inv_kappa = 1.0


def pieces_of(band):
    out = []
    hop, left = 1, REACH
    while left > 0:
        n = min(band, left)
        out.append((hop, band - n, n, -(hop - 1) * band - n))
        out.append((-hop, 0, n, hop * band))
        left -= n
        hop += 1
    return out


def constants_of(species, band):
    pieces = pieces_of(band)
    rows_d = species * band
    picked = [(k, first + p) for _, first, n, _ in pieces for k in range(species) for p in range(n)]
    pick = np.zeros((-(-len(picked) // 8) * 8, rows_d), np.float32)
    for i, (k, z) in enumerate(picked):
        pick[i, k * band + z] = 1.0
    source = [(k, z) for k in range(species) for z in range(band)]
    source += [(k, at + p) for _, _, n, at in pieces for k in range(species) for p in range(n)]
    rows_v = -(-len(source) // 16) * 16
    left = np.zeros((2 * rows_d, species), np.float32)
    right = np.zeros((species, rows_v), np.float32)
    along_z = np.zeros((2 * rows_d, rows_v), np.float32)
    off_diag = np.zeros((2 * rows_d, rows_v), np.float32)
    tap = lambda t: taps[t + 2] if -2 <= t <= 2 else 0.0
    for kind in range(2):
        for k in range(species):
            for z in range(band):
                i = kind * rows_d + k * band + z
                left[i, k] = 1.0
                for j, (l, at) in enumerate(source):
                    right[l, j] = 1.0
                    off_diag[i, j] = float(k != l)
                    value = tap(at - z) if kind == 0 else tap(at - z - 1) - tap(at - z + 1)
                    along_z[i, j] = -0.5 * value
    return pick.astype(jnp.bfloat16), left, right, along_z, off_diag


def exact(a, b, dims=(((1,), (0,)), ((), ()))):
    return lax.dot_general(a, b, dims, precision=lax.Precision.HIGHEST, preferred_element_type=jnp.float32)


def fill_weights(species_ref, mix_ref, wts):
    for k in range(wts.shape[0]):
        onehot = (species_ref[0] == k).astype(jnp.float32)
        wts[k] = (onehot + mix_ref[0, k].astype(jnp.float32)).astype(jnp.bfloat16).astype(jnp.float32)


def banded_of(cells, count, wts, d, first_z, band):
    slots = cells.shape[1]
    z = (cells & (NZ - 1)) - first_z
    z = jnp.where(lax.broadcasted_iota(jnp.int32, (1, slots), 1) < count, z, -1)
    hit = z == lax.broadcasted_iota(jnp.int32, (band, slots), 0)
    parts = [jnp.where(hit, wts[k, pl.ds(d, 1), :], 0.0) for k in range(wts.shape[0])]
    return jnp.concatenate(parts, axis=0)


def table_of(cells):
    plane = lax.shift_right_logical(cells, NZ.bit_length() - 1)
    ids = lax.broadcasted_iota(jnp.int32, (BX * BY, cells.shape[1]), 0)
    return jnp.where(plane == ids, 1.0, 0.0).astype(jnp.bfloat16)


def deposit_kernel(n_col, band, first_ref, counts_ref, cells_ref, species_ref, mix_ref, pick_ref, *refs):
    pieces = pieces_of(band)
    dens_ref, sends, stages, wts = refs[0], refs[1:1 + len(pieces)], refs[1 + len(pieces):1 + 2 * len(pieces)], refs[-1]
    count = wts.shape[0]
    fill_weights(species_ref, mix_ref, wts)
    first_z = first_ref[0]

    def one_row(r, carry):
        for q in range(n_col):
            d = r * n_col + q
            cells = cells_ref[0, pl.ds(d, 1), :]
            banded = banded_of(cells, counts_ref[0, d], wts, d, first_z, band)
            tile = lax.dot_general(
                banded.astype(jnp.bfloat16), table_of(cells), (((1,), (1,)), ((), ())),
                preferred_element_type=jnp.float32,
            )
            dens_ref[2 * r, q] = tile[:, :LANES]
            dens_ref[2 * r + 1, q] = tile[:, LANES:]
            edge = jnp.dot(pick_ref[...], tile.astype(jnp.bfloat16), preferred_element_type=jnp.float32)
            at = 0
            for stage, (_, _, n, _) in zip(stages, pieces):
                rows = n * count
                stage[q * rows:(q + 1) * rows, :] = edge[at:at + rows]
                at += rows
        for send, stage in zip(sends, stages):
            send[r] = stage[...].astype(jnp.bfloat16)
        return carry

    lax.fori_loop(0, dens_ref.shape[0] // 2, one_row, 0)


def lane_of(rows):
    return lax.broadcasted_iota(jnp.int32, (rows, LANES), 1)


def roll(value, shift):
    return pltpu.roll(value, shift % LANES, 1)


def moved_y(before, here, after, lane_y, t):
    if t > 0:
        return jnp.where(lane_y < BY - t, roll(here, -t), roll(after, BY - t))
    return jnp.where(lane_y >= -t, roll(here, -t), roll(before, -BY - t))


def moved_x(before, here, after, lane_x, t):
    if t > 0:
        return jnp.where(lane_x < HALF - t, roll(here, -t * BY), roll(after, -t * BY))
    return jnp.where(lane_x >= -t, roll(here, -t * BY), roll(before, -t * BY))


def smoothed(moved, before, here, after, lane):
    total = taps[2] * here
    for t in (1, 2):
        total = total + taps[2 + t] * (moved(before, here, after, lane, t) + moved(before, here, after, lane, -t))
    return total


def force_kernel(n_col, band, first_ref, counts_ref, cells_ref, species_ref, mix_ref, chi_ref, left_ref, right_ref,
                 along_ref, off_ref, dens_ref, *refs):
    pieces = pieces_of(band)
    recvs = refs[:len(pieces)]
    out_ref, wts, raw, half_done, fields, maps = refs[len(pieces):]
    count = wts.shape[0]
    rows_d = count * band
    halves, rows_v = raw.shape[0], raw.shape[2]
    rows_m = maps.shape[1]
    first_z = first_ref[0]
    fill_weights(species_ref, mix_ref, wts)

    chi = chi_ref[...]
    mixing = exact(exact(left_ref[...], chi), right_ref[...])
    mixing += exact(exact(left_ref[...], chi, (((1,), (1,)), ((), ()))), right_ref[...])
    mixing = (mixing * (0.5 / rho_ref)) * off_ref[...] + inv_kappa / rho_ref
    full = mixing * along_ref[...]
    high = full.astype(jnp.bfloat16)
    maps[:2 * rows_d] = high
    maps[2 * rows_d:] = (full - high.astype(jnp.float32)).astype(jnp.bfloat16)

    def spread(r, carry):
        got = [recv[r].astype(jnp.float32) for recv in recvs]
        for q in range(n_col):
            parts = [part[q * n * count:(q + 1) * n * count] for part, (_, _, n, _) in zip(got, pieces)]
            used = rows_d + 2 * REACH * count
            edge = jnp.concatenate(parts, axis=0)
            for h in range(2):
                raw[2 * r + h, q, :rows_d] = dens_ref[2 * r + h, q]
                raw[2 * r + h, q, rows_d:used] = edge[:, h * LANES:(h + 1) * LANES]
                if rows_v > used:
                    raw[2 * r + h, q, used:] = jnp.zeros((rows_v - used, LANES), jnp.float32)
        return carry

    lax.fori_loop(0, halves // 2, spread, 0)

    def smooth_y(i, carry):
        h, q = i // n_col, i % n_col
        lane = lane_of(rows_v) % BY
        half_done[h, q] = smoothed(
            moved_y, raw[h, (q + n_col - 1) % n_col], raw[h, q], raw[h, (q + 1) % n_col], lane
        )
        return carry

    lax.fori_loop(0, halves * n_col, smooth_y, 0)

    def smooth_x(i, carry):
        r, q = i // n_col, i % n_col
        lane = lane_of(rows_v) // BY
        a, b = half_done[(2 * r + halves - 1) % halves, q], half_done[2 * r, q]
        c, d = half_done[2 * r + 1, q], half_done[(2 * r + 2) % halves, q]
        value = jnp.concatenate(
            [smoothed(moved_x, a, b, c, lane), smoothed(moved_x, b, c, d, lane)], axis=1
        )
        if rows_m > rows_v:
            value = jnp.concatenate([value, jnp.zeros((rows_m - rows_v, 2 * LANES), jnp.float32)], axis=0)
        top = value.astype(jnp.bfloat16)
        rest = (value - top.astype(jnp.float32)).astype(jnp.bfloat16)
        first = jnp.dot(maps[...], top, preferred_element_type=jnp.float32)
        field = first[:2 * rows_d] + first[2 * rows_d:]
        field = field + jnp.dot(maps[:2 * rows_d], rest, preferred_element_type=jnp.float32)
        fields[2 * r, q] = field[:, :LANES]
        fields[2 * r + 1, q] = field[:, LANES:]
        return carry

    lax.fori_loop(0, halves // 2 * n_col, smooth_x, 0)

    def gather(d, carry):
        r, q = d // n_col, d % n_col
        lane = lane_of(rows_d)
        lane_x, lane_y = lane // BY, lane % BY
        parts = []
        for h in range(2):
            at = 2 * r + h
            here = fields[at, q, :rows_d]
            back, on = fields[(at + halves - 1) % halves, q, :rows_d], fields[(at + 1) % halves, q, :rows_d]
            grad_x = moved_x(back, here, on, lane_x, 1) - moved_x(back, here, on, lane_x, -1)
            back, on = fields[at, (q + n_col - 1) % n_col, :rows_d], fields[at, (q + 1) % n_col, :rows_d]
            grad_y = moved_y(back, here, on, lane_y, 1) - moved_y(back, here, on, lane_y, -1)
            parts.append((grad_x, grad_y, fields[at, q, rows_d:]))
        cells = cells_ref[0, pl.ds(d, 1), :]
        table = table_of(cells)
        banded = banded_of(cells, counts_ref[0, d], wts, d, first_z, band)
        for a in range(3):
            grad = jnp.concatenate([parts[0][a], parts[1][a]], axis=1)
            top = grad.astype(jnp.bfloat16)
            rest = (grad - top.astype(jnp.float32)).astype(jnp.bfloat16)
            value = jnp.dot(top, table, preferred_element_type=jnp.float32)
            value = value + jnp.dot(rest, table, preferred_element_type=jnp.float32)
            out_ref[0, a, pl.ds(d, 1), :] = jnp.sum(value * banded, axis=0, keepdims=True)
        return carry

    lax.fori_loop(0, halves // 2 * n_col, gather, 0)


def body(n_row, n_col, send_cells, send_species, send_mix, send_counts, chi):
    species, domains, slots = send_mix.shape[1:]
    band = NZ // domains
    halves = 2 * n_row
    rows_d = species * band
    pieces = pieces_of(band)
    pick, left, right, along_z, off_diag = constants_of(species, band)
    rows_v = -(-(rows_d + 2 * REACH * species) // 8) * 8
    first = ((lax.axis_index("row") * n_col + lax.axis_index("col")) * band).astype(jnp.int32)[None]
    smem, vmem = pl.BlockSpec(memory_space=pltpu.SMEM), pl.BlockSpec(memory_space=pltpu.VMEM)
    params = pltpu.CompilerParams(vmem_limit_bytes=48 * 2**20)
    edge_rows = [n_col * n * species for _, _, n, _ in pieces]
    made = pl.pallas_call(
        functools.partial(deposit_kernel, n_col, band),
        out_shape=[jax.ShapeDtypeStruct((halves, n_col, rows_d, LANES), jnp.float32)]
        + [jax.ShapeDtypeStruct((n_row, rows, BX * BY), jnp.bfloat16) for rows in edge_rows],
        in_specs=[smem, smem] + [vmem] * 4,
        out_specs=[vmem] * (1 + len(pieces)),
        scratch_shapes=[pltpu.VMEM((rows, BX * BY), jnp.float32) for rows in edge_rows]
        + [pltpu.VMEM((species, domains, slots), jnp.float32)],
        compiler_params=params,
        name="deposit",
    )(first, send_counts, send_cells, send_species, send_mix, pick)
    dens, sends = made[0], made[1:]
    recvs = [
        lax.ppermute(send, ("row", "col"), [(i, (i + hop) % domains) for i in range(domains)])
        for send, (hop, _, _, _) in zip(sends, pieces)
    ]
    return pl.pallas_call(
        functools.partial(force_kernel, n_col, band),
        out_shape=jax.ShapeDtypeStruct((1, 3, domains, slots), jnp.float32),
        in_specs=[smem, smem] + [vmem] * (9 + len(pieces)),
        out_specs=vmem,
        scratch_shapes=[
            pltpu.VMEM((species, domains, slots), jnp.float32),
            pltpu.VMEM((halves, n_col, rows_v, LANES), jnp.float32),
            pltpu.VMEM((halves, n_col, rows_v, LANES), jnp.float32),
            pltpu.VMEM((halves, n_col, 2 * rows_d, LANES), jnp.float32),
            pltpu.VMEM((4 * rows_d, along_z.shape[1]), jnp.bfloat16),
        ],
        compiler_params=params,
        name="force",
    )(first, send_counts, send_cells, send_species, send_mix, chi, left, right, along_z, off_diag, dens, *recvs)


def solution(mesh):
    spec = P(("row", "col"))
    return jax.shard_map(
        functools.partial(body, mesh.shape["row"], mesh.shape["col"]),
        mesh=mesh,
        in_specs=(spec, spec, spec, spec, P()),
        out_specs=spec,
        check_vma=False,
    )
```

time: 199 us -> 74.4 us (0.37)
  local copies, waits for them, and re-layouts: 91 us -> 7.73 us
  Pallas kernels: 0 us -> 48.3 us
  matrix products: 29.8 us -> 0 us
  waiting for transfers between devices: 28 us -> 11.3 us
  other arithmetic: 15.4 us -> 0 us
  blocking collectives: 13.8 us -> 0 us
  starting transfers between devices: 19 us -> 6.49 us
    another operation x4 -> x0, local copies, waits for them, and re-layouts: 60.6 us -> none  [the longest x1 26.4 us: pick_forces(): grads.reshape(3 * SPECIES, plane, sources, band)]
    pallas_call x0 -> x2, Pallas kernels: none -> 48.3 us  [the longest x1 39.2 us: body(): pl.pallas_call(functools.partial(force_kernel, n_col, band), out_shape=ja...]
    dot_general x9 -> x0, matrix products: 29.8 us -> none  [the longest x4 17.7 us: pick_one_block(): jnp.einsum('bjzc,bpc->bjzp', g_b, table, precision=lax.Precision.HIGHEST)]
    slice x11 -> x0, local copies, waits for them, and re-layouts: 15.7 us -> none  [the longest x3 8.27 us: extended_2(): last = lax.slice_in_dim(value, length - width, length, axis=dim)]
    all_to_all x2 -> x0, waiting for transfers between devices: 15.2 us -> none  [the longest x1 10.5 us: body(): lax.all_to_all(weights, ('row', 'col'), split_axis=1, concat_axis=1, tile...]
    all_to_all x1 -> x0, blocking collectives: 13.8 us -> none  [body(): lax.all_to_all(slot_forces, ('row', 'col'), split_axis=1, concat_axis=1,...]
    all_to_all x2 -> x0, starting transfers between devices: 9.88 us -> none  [the longest x1 7.3 us: body(): lax.all_to_all(send_cells, ('row', 'col'), split_axis=1, concat_axis=1, t...]
    concatenate x3 -> x0, local copies, waits for them, and re-layouts: 7.62 us -> none  [body(): grad_z = 0.5 * (jnp.roll(center, -1, axis=3) - jnp.roll(center, 1, axis=3))]
  transfers between devices with their start and end apart: 10 -> 2, of which waited for: 6 -> 2; matrix products, arithmetic and copies ran while one was open for 13% -> 0% of each run, Pallas kernels for 0% -> 0%
where the time goes in v1:
time: 74.4 us; the launch traced here: 73.9 us
  Pallas kernels  48.3 us (65%)
  waiting for transfers between devices  11.3 us (15%)
  local copies, waits for them, and re-layouts  7.73 us (10%)
  starting transfers between devices  6.49 us (9%)
    pallas_call x1, Pallas kernels, body(): pl.pallas_call(functools.partial(force_kernel, n_col, band), out_shape=ja...  39.2 us
    ppermute x2, waiting for transfers between devices, body(): lax.ppermute(send, ('row', 'col'), [(i, (i + hop) % domains) for i in ran...  11.3 us
    pallas_call x1, Pallas kernels, body(): pl.pallas_call(functools.partial(deposit_kernel, n_col, band), out_shape=...  9.16 us
    unnamed x20, local copies, waits for them, and re-layouts  7.73 us
    ppermute x2, starting transfers between devices, body(): lax.ppermute(send, ('row', 'col'), [(i, (i + hop) % domains) for i in ran...  6.49 us
  transfers between devices with their start and end apart: 2, of which 2 were waited for; matrix products, arithmetic and copies ran while one was open for 0% of the time, Pallas kernels for 0%

profile of v1, /device:TPU:0, one launch (start us, length us, event | category | flops | bytes accessed | tf_op | source)
XLA Modules:
  0.0 73.9 jit_solution(6890630272122056440)
XLA Ops:
  0.0 0.0 copy-start
  0.0 0.9 %copy-done = bf16[1,6,32,512]{3,2,1,0:T(8,128)(2,1)S(1)} copy-done((bf16[1,6,32,512]{3,2,1,0:T(8,128)(2,1)S(1)}, bf16[1,6,32,512]{3,2,1,0:T(8,128)(2,1)}, u32[]{:S(2)}) %copy-start) | copy-done | bytes 196632
  0.9 0.0 copy-start.1
  0.9 0.8 %copy-done.1 = s32[1,32,512]{2,1,0:T(8,128)S(1)} copy-done((s32[1,32,512]{2,1,0:T(8,128)S(1)}, s32[1,32,512]{2,1,0:T(8,128)}, u32[]{:S(2)}) %copy-start.1) | copy-done | bytes 65560
  1.8 0.0 copy-start.2
  1.8 0.8 %copy-done.2 = s32[1,32,512]{2,1,0:T(8,128)S(1)} copy-done((s32[1,32,512]{2,1,0:T(8,128)S(1)}, s32[1,32,512]{2,1,0:T(8,128)}, u32[]{:S(2)}) %copy-start.2) | copy-done | bytes 65560
  2.6 0.0 copy-start.6
  2.6 0.7 copy-done.6
  3.3 0.0 copy-start.9
  3.3 0.7 copy-done.9
  4.0 9.2 %deposit.1 = (f32[8,8,48,128]{3,2,1,0:T(8,128)S(1)}, bf16[4,144,256]{2,1,0:T(8,128)(2,1)S(1)}, bf16[4,144,256]{2,1,0:T(8,128)(2,1)S(1)}) custom-call(s32[1]{0:T(128)} %bitcast.first_ref, s32[1,32]{1,0:T(1,128)S(1)} %copy-done.9, s32[1,32,512]{2,1,0:T(8,128)S(1)} %copy-done.1, s32[1,32,512]{2,1,0:T(8,128)S(1)} %copy-done.2, ...), custom_call_target="tpu_custom_call" | custom-call | tf_op jit(solution)/shard_map/deposit/pallas_call | solution.py:255
  13.1 3.0 %collective-permute-start = (bf16[4,144,256]{2,1,0:T(8,128)(2,1)S(1)}, bf16[4,144,256]{2,1,0:T(8,128)(2,1)S(1)}, u32[]{:S(2)}, u32[]{:S(2)}) collective-permute-start(bf16[4,144,256]{2,1,0:T(8,128)(2,1)S(1)} %get-tuple-element.9), channel_id=1, source_target_pairs={{0,1},{1,2},{2,3},{3,4},{4,5},{5,6},{6,7},{7,8},{8,9},{9,10},{10,1... | collective-permute-start | bytes 884744 | tf_op jit(solution)/shard_map/ppermute | solution.py:268
  16.2 3.5 %collective-permute-start.1 = (bf16[4,144,256]{2,1,0:T(8,128)(2,1)S(1)}, bf16[4,144,256]{2,1,0:T(8,128)(2,1)S(1)}, u32[]{:S(2)}, u32[]{:S(2)}) collective-permute-start(bf16[4,144,256]{2,1,0:T(8,128)(2,1)S(1)} %get-tuple-element.10), channel_id=1, source_target_pairs={{0,31},{1,0},{2,1},{3,2},{4,3},{5,4},{6,5},{7,6},{8,7},{9,8},{10,9... | collective-permute-start | bytes 884744 | tf_op jit(solution)/shard_map/ppermute | solution.py:268
  19.6 9.1 %collective-permute-done.refs_0_ = bf16[4,144,256]{2,1,0:T(8,128)(2,1)S(1)} collective-permute-done((bf16[4,144,256]{2,1,0:T(8,128)(2,1)S(1)}, bf16[4,144,256]{2,1,0:T(8,128)(2,1)S(1)}, u32[]{:S(2)}, u32[]{:S(2)}) %collective-permute-start) | collective-permute-done | bytes 294944 | tf_op jit(solution)/shard_map/ppermute | solution.py:268
  28.7 2.2 %collective-permute-done.1.refs_1_ = bf16[4,144,256]{2,1,0:T(8,128)(2,1)S(1)} collective-permute-done((bf16[4,144,256]{2,1,0:T(8,128)(2,1)S(1)}, bf16[4,144,256]{2,1,0:T(8,128)(2,1)S(1)}, u32[]{:S(2)}, u32[]{:S(2)}) %collective-permute-start.1) | collective-permute-done | bytes 294944 | tf_op jit(solution)/shard_map/ppermute | solution.py:268
  30.9 0.0 copy-start.3
  31.0 0.8 %copy-done.3 = f32[96,96]{1,0:T(8,128)S(1)} copy-done((f32[96,96]{1,0:T(8,128)S(1)}, f32[96,96]{1,0:T(8,128)}, u32[]{:S(2)}) %copy-start.3) | copy-done | bytes 36888
  31.7 0.0 copy-start.4
  31.8 0.8 %copy-done.4 = f32[96,96]{1,0:T(8,128)S(1)} copy-done((f32[96,96]{1,0:T(8,128)S(1)}, f32[96,96]{1,0:T(8,128)}, u32[]{:S(2)}) %copy-start.4) | copy-done | bytes 36888
  32.5 0.0 copy-start.5
  32.5 0.8 %copy-done.5 = f32[96,6]{1,0:T(8,128)S(1)} copy-done((f32[96,6]{1,0:T(8,128)S(1)}, f32[96,6]{1,0:T(8,128)}, u32[]{:S(2)}) %copy-start.5) | copy-done | bytes 2328
  33.3 0.0 copy-start.7
  33.3 0.7 copy-done.7
  34.0 0.0 copy-start.8
  34.0 0.7 copy-done.8
  34.7 39.2 %force.1 = f32[1,3,32,512]{3,2,1,0:T(8,128)} custom-call(s32[1]{0:T(128)} %bitcast.first_ref, s32[1,32]{1,0:T(1,128)S(1)} %copy-done.9, s32[1,32,512]{2,1,0:T(8,128)S(1)} %copy-done.1, s32[1,32,512]{2,1,0:T(8,128)S(1)} %copy-done.2, bf16[1,6,32,512]{3,2,1,0:T(8,128)(2,1)S(1)} %copy-done, f32[6,6]{1,0:T(8,128)S(1)} %copy-done.7, f32[96,6]{1,0:T(8,128)S(1)} %copy-done.5, ...), custom_call_target="tpu_custom_call" | custom-call | tf_op jit(solution)/shard_map/force/pallas_call | solution.py:271
Async XLA Ops:
  0.0 0.9 %copy-start = (bf16[1,6,32,512]{3,2,1,0:T(8,128)(2,1)S(1)}, bf16[1,6,32,512]{3,2,1,0:T(8,128)(2,1)}, u32[]{:S(2)}) copy-start(bf16[1,6,32,512]{3,2,1,0:T(8,128)(2,1)} %mix_ref.3) | copy-start | bytes 589828
  0.9 0.8 %copy-start.1 = (s32[1,32,512]{2,1,0:T(8,128)S(1)}, s32[1,32,512]{2,1,0:T(8,128)}, u32[]{:S(2)}) copy-start(s32[1,32,512]{2,1,0:T(8,128)} %cells_ref.3) | copy-start | bytes 196612
  1.8 0.8 %copy-start.2 = (s32[1,32,512]{2,1,0:T(8,128)S(1)}, s32[1,32,512]{2,1,0:T(8,128)}, u32[]{:S(2)}) copy-start(s32[1,32,512]{2,1,0:T(8,128)} %species_ref.3) | copy-start | bytes 196612
  2.6 0.7 copy-start.6
  3.3 0.7 copy-start.9
  13.1 15.6 %collective-permute-start = (bf16[4,144,256]{2,1,0:T(8,128)(2,1)S(1)}, bf16[4,144,256]{2,1,0:T(8,128)(2,1)S(1)}, u32[]{:S(2)}, u32[]{:S(2)}) collective-permute-start(bf16[4,144,256]{2,1,0:T(8,128)(2,1)S(1)} %get-tuple-element.9), channel_id=1, source_target_pairs={{0,1},{1,2},{2,3},{3,4},{4,5},{5,6},{6,7},{7,8},{8,9},{9,10},{10,1... | collective-permute-start | bytes 884744 | tf_op jit(solution)/shard_map/ppermute | solution.py:268
  16.2 14.8 %collective-permute-start.1 = (bf16[4,144,256]{2,1,0:T(8,128)(2,1)S(1)}, bf16[4,144,256]{2,1,0:T(8,128)(2,1)S(1)}, u32[]{:S(2)}, u32[]{:S(2)}) collective-permute-start(bf16[4,144,256]{2,1,0:T(8,128)(2,1)S(1)} %get-tuple-element.10), channel_id=1, source_target_pairs={{0,31},{1,0},{2,1},{3,2},{4,3},{5,4},{6,5},{7,6},{8,7},{9,8},{10,9... | collective-permute-start | bytes 884744 | tf_op jit(solution)/shard_map/ppermute | solution.py:268
  30.9 0.8 %copy-start.3 = (f32[96,96]{1,0:T(8,128)S(1)}, f32[96,96]{1,0:T(8,128)}, u32[]{:S(2)}) copy-start(f32[96,96]{1,0:T(8,128)} %constant.24.clone.off_ref) | copy-start | bytes 110596
  31.7 0.8 %copy-start.4 = (f32[96,96]{1,0:T(8,128)S(1)}, f32[96,96]{1,0:T(8,128)}, u32[]{:S(2)}) copy-start(f32[96,96]{1,0:T(8,128)} %constant.23.clone.along_ref) | copy-start | bytes 110596
  32.5 0.8 %copy-start.5 = (f32[96,6]{1,0:T(8,128)S(1)}, f32[96,6]{1,0:T(8,128)}, u32[]{:S(2)}) copy-start(f32[96,6]{1,0:T(8,128)} %constant.21.clone.left_ref) | copy-start | bytes 6916
  33.3 0.7 copy-start.7
  34.0 0.7 copy-start.8

commit v2 on v1

v2 whole, which is shorter than its diff:
```python
import functools

import jax
import jax.numpy as jnp
import numpy as np
from jax import lax
from jax.experimental import pallas as pl
from jax.experimental.pallas import tpu as pltpu
from jax.sharding import PartitionSpec as P

BX = 16
BY = 16
NZ = 256
LANES = 128
HALF = LANES // BY
REACH = 3

raw_taps = (0.1353352832366127, 0.6065306597126334, 1.0, 0.6065306597126334, 0.1353352832366127)
tap_total = sum(raw_taps)
taps = tuple(t / tap_total for t in raw_taps)
rho_ref = 2.0
inv_kappa = 1.0


def pieces_of(band):
    out = []
    hop, left = 1, REACH
    while left > 0:
        n = min(band, left)
        out.append((hop, band - n, n, -(hop - 1) * band - n))
        out.append((-hop, 0, n, hop * band))
        left -= n
        hop += 1
    return out


def constants_of(species, band):
    pieces = pieces_of(band)
    rows_d = species * band
    rows_h = -(-2 * REACH * species // 8) * 8
    source = [(k, z) for k in range(species) for z in range(band)]
    source += [(k, at + p) for _, _, n, at in pieces for k in range(species) for p in range(n)]
    rows_m = -(-(rows_d + rows_h) // 16) * 16
    left = np.zeros((2 * rows_d, species), np.float32)
    right = np.zeros((species, rows_m), np.float32)
    along_z = np.zeros((2, 2 * rows_d, rows_m), np.float32)
    tap = lambda t: taps[t + 2] if -2 <= t <= 2 else 0.0
    for kind in range(2):
        for k in range(species):
            for z in range(band):
                i = kind * rows_d + k * band + z
                left[i, k] = 1.0
                for j, (l, at) in enumerate(source):
                    right[l, j] = 1.0
                    value = tap(at - z) if kind == 0 else tap(at - z - 1) - tap(at - z + 1)
                    along_z[0, i, j] = -0.5 * value * (0.5 / rho_ref) * float(k != l)
                    along_z[1, i, j] = -0.5 * value * (inv_kappa / rho_ref)
    return left, right, along_z


def exact(a, b, dims=(((1,), (0,)), ((), ()))):
    return lax.dot_general(a, b, dims, precision=lax.Precision.HIGHEST, preferred_element_type=jnp.float32)


def fill_weights(species_ref, mix_ref, wts):
    for k in range(wts.shape[0]):
        onehot = (species_ref[0] == k).astype(jnp.float32)
        wts[k] = (onehot + mix_ref[0, k].astype(jnp.float32)).astype(jnp.bfloat16).astype(jnp.float32)


def banded_of(cells, count, wts, d, first_z, band):
    slots = cells.shape[1]
    z = (cells & (NZ - 1)) - first_z
    z = jnp.where(lax.broadcasted_iota(jnp.int32, (1, slots), 1) < count, z, -1)
    hit = z == lax.broadcasted_iota(jnp.int32, (band, slots), 0)
    parts = [jnp.where(hit, wts[k, pl.ds(d, 1), :], 0.0) for k in range(wts.shape[0])]
    return jnp.concatenate(parts, axis=0)


def table_of(cells):
    plane = lax.shift_right_logical(cells, NZ.bit_length() - 1)
    ids = lax.broadcasted_iota(jnp.int32, (BX * BY, cells.shape[1]), 0)
    return jnp.where(plane == ids, 1.0, 0.0).astype(jnp.bfloat16)


def chunks_of(rows):
    return [(at, min(8, rows - at)) for at in range(0, rows, 8)]


def lane_of(rows):
    return lax.broadcasted_iota(jnp.int32, (rows, LANES), 1)


def lane_x_of(rows):
    return lax.shift_right_logical(lane_of(rows), BY.bit_length() - 1)


def lane_y_of(rows):
    return lane_of(rows) & (BY - 1)


def roll(value, shift):
    return pltpu.roll(value, shift % LANES, 1)


def moved_y(ahead, here, lane_y, t):
    if t > 0:
        return roll(jnp.where(lane_y < t, ahead, here), -t)
    return roll(jnp.where(lane_y >= BY + t, ahead, here), -t)


def moved_x(ahead, here, lane_x, t):
    if t > 0:
        return roll(jnp.where(lane_x < t, ahead, here), -t * BY)
    return roll(jnp.where(lane_x >= HALF + t, ahead, here), -t * BY)


def smoothed(moved, before, here, after, lane):
    one = moved(after, here, lane, 1) + moved(before, here, lane, -1)
    two = moved(after, here, lane, 2) + moved(before, here, lane, -2)
    return taps[2] * here + taps[3] * one + taps[4] * two


def smooth_y(src, dst, h, n_col):
    for at, size in chunks_of(src.shape[2]):
        lane_y = lane_y_of(size)
        rows = [src[h, q, at:at + size] for q in range(n_col)]
        for q in range(n_col):
            before, after = roll(rows[q - 1], -BY), roll(rows[(q + 1) % n_col], BY)
            dst[h, q, at:at + size] = smoothed(moved_y, before, rows[q], after, lane_y)


def smooth_x(src, r, q):
    halves = src.shape[0]
    out = ([], [])
    for at, size in chunks_of(src.shape[2]):
        lane_x = lane_x_of(size)
        a, b = src[(2 * r + halves - 1) % halves, q, at:at + size], src[2 * r, q, at:at + size]
        c, d = src[2 * r + 1, q, at:at + size], src[(2 * r + 2) % halves, q, at:at + size]
        out[0].append(smoothed(moved_x, a, b, c, lane_x))
        out[1].append(smoothed(moved_x, b, c, d, lane_x))
    return out


def membrane_kernel(n_row, n_col, band, counts_ref, cells_hbm, species_hbm, mix_hbm, chi_hbm, left_hbm, right_hbm,
                    along_hbm, out_ref, *refs):
    pieces = pieces_of(band)
    held, refs = refs[:7], refs[7:]
    sends, refs = refs[:len(pieces)], refs[len(pieces):]
    recvs, refs = refs[:len(pieces)], refs[len(pieces):]
    stages, refs = refs[:len(pieces)], refs[len(pieces):]
    wts, raw, turned, edge_raw, edge_turned, fields, maps, load_sem, send_sem, recv_sem = refs
    cells_ref, species_ref, mix_ref, chi_ref, left_ref, right_ref, along_ref = held
    count = wts.shape[0]
    rows_d, rows_h = count * band, edge_raw.shape[2]
    halves, rows_m = 2 * n_row, maps.shape[1]
    bricks = n_row * n_col
    me = lax.axis_index("row") * n_col + lax.axis_index("col")
    first_z = me * band

    loads = [
        pltpu.make_async_copy(src, dst, load_sem.at[i])
        for i, (src, dst) in enumerate(
            zip((cells_hbm, species_hbm, mix_hbm, chi_hbm, left_hbm, right_hbm, along_hbm), held)
        )
    ]
    for load in loads:
        load.start()

    def device_at(hop):
        there = (me + hop + bricks) % bricks
        return (there // n_col, there % n_col)

    barrier = pltpu.get_barrier_semaphore()
    for hop, _, _, _ in pieces:
        pl.semaphore_signal(barrier, inc=1, device_id=device_at(hop), device_id_type=pl.DeviceIdType.MESH)

    def transfer(i, r):
        return pltpu.make_async_remote_copy(
            src_ref=sends[i].at[r],
            dst_ref=recvs[i].at[r],
            send_sem=send_sem.at[i, r],
            recv_sem=recv_sem.at[i, r],
            device_id=device_at(pieces[i][0]),
            device_id_type=pl.DeviceIdType.MESH,
        )

    for load in loads[:3]:
        load.wait()
    fill_weights(species_ref, mix_ref, wts)
    used = 2 * REACH * count
    if rows_h > used:
        edge_raw[:, :, used:] = jnp.zeros((halves, n_col, rows_h - used, LANES), jnp.float32)
    pl.semaphore_wait(barrier, len(pieces))

    def deposit(r, carry):
        for q in range(n_col):
            d = r * n_col + q
            cells = cells_ref[0, pl.ds(d, 1), :]
            banded = banded_of(cells, counts_ref[0, d], wts, d, first_z, band)
            tile = lax.dot_general(
                banded.astype(jnp.bfloat16), table_of(cells), (((1,), (1,)), ((), ())),
                preferred_element_type=jnp.float32,
            )
            raw[2 * r, q] = tile[:, :LANES]
            raw[2 * r + 1, q] = tile[:, LANES:]
            for stage, (_, first, n, _) in zip(stages, pieces):
                for k in range(count):
                    to = (q * count + k) * n
                    stage[to:to + n, :] = tile[k * band + first:k * band + first + n]
        for i in range(len(pieces)):
            sends[i][r] = stages[i][...].astype(jnp.bfloat16)
            transfer(i, r).start()
        return carry

    lax.fori_loop(0, n_row, deposit, 0)

    for load in loads[3:]:
        load.wait()
    chi = chi_ref[...]
    mixing = exact(exact(left_ref[...], chi), right_ref[...])
    mixing += exact(exact(left_ref[...], chi, (((1,), (1,)), ((), ()))), right_ref[...])
    full = mixing * along_ref[0] + along_ref[1]
    high = full.astype(jnp.bfloat16)
    maps[:2 * rows_d] = high
    maps[2 * rows_d:] = (full - high.astype(jnp.float32)).astype(jnp.bfloat16)

    def inner_y(h, carry):
        smooth_y(raw, turned, h, n_col)
        return carry

    lax.fori_loop(0, halves, inner_y, 0)

    def inner_x(d, carry):
        r, q = d // n_col, d % n_col
        for h, done in enumerate(smooth_x(turned, r, q)):
            for (at, size), value in zip(chunks_of(rows_d), done):
                raw[2 * r + h, q, at:at + size] = value
        return carry

    lax.fori_loop(0, bricks, inner_x, 0, unroll=2)

    def edge_y(r, carry):
        for i in range(len(pieces)):
            transfer(i, r).wait_recv()
        got = [recv[r].astype(jnp.float32) for recv in recvs]
        for q in range(n_col):
            at = 0
            for part, (_, _, n, _) in zip(got, pieces):
                rows = n * count
                for h in range(2):
                    edge_raw[2 * r + h, q, at:at + rows] = part[q * rows:(q + 1) * rows, h * LANES:(h + 1) * LANES]
                at += rows
        for h in range(2):
            smooth_y(edge_raw, edge_turned, 2 * r + h, n_col)
        return carry

    lax.fori_loop(0, n_row, edge_y, 0)

    def to_fields(d, carry):
        r, q = d // n_col, d % n_col
        done = []
        for h, edges in enumerate(smooth_x(edge_turned, r, q)):
            parts = [raw[2 * r + h, q]] + edges
            if rows_m > rows_d + rows_h:
                parts.append(jnp.zeros((rows_m - rows_d - rows_h, LANES), jnp.float32))
            done.append(jnp.concatenate(parts, axis=0))
        value = jnp.concatenate(done, axis=1)
        top = value.astype(jnp.bfloat16)
        rest = (value - top.astype(jnp.float32)).astype(jnp.bfloat16)
        first = jnp.dot(maps[...], top, preferred_element_type=jnp.float32)
        field = first[:2 * rows_d] + first[2 * rows_d:]
        field = field + jnp.dot(maps[:2 * rows_d], rest, preferred_element_type=jnp.float32)
        fields[2 * r, q] = field[:, :LANES]
        fields[2 * r + 1, q] = field[:, LANES:]
        return carry

    lax.fori_loop(0, bricks, to_fields, 0, unroll=2)

    def gather(d, carry):
        r, q = d // n_col, d % n_col
        grads = ([], [], [])
        for at, size in chunks_of(rows_d):
            lane_x, lane_y = lane_x_of(size), lane_y_of(size)
            sides = ([], [])
            for h in range(2):
                half = 2 * r + h
                here = fields[half, q, at:at + size]
                back, on = (fields[(half + step + halves) % halves, q, at:at + size] for step in (-1, 1))
                sides[0].append(moved_x(on, here, lane_x, 1) - moved_x(back, here, lane_x, -1))
                back, on = (fields[half, (q + step + n_col) % n_col, at:at + size] for step in (-1, 1))
                back, on = roll(back, -BY), roll(on, BY)
                sides[1].append(moved_y(on, here, lane_y, 1) - moved_y(back, here, lane_y, -1))
            for a in range(2):
                grads[a].append(jnp.concatenate(sides[a], axis=1))
        grads[2].append(
            jnp.concatenate([fields[2 * r, q, rows_d:], fields[2 * r + 1, q, rows_d:]], axis=1)
        )
        grad = jnp.concatenate(grads[0] + grads[1] + grads[2], axis=0)
        cells = cells_ref[0, pl.ds(d, 1), :]
        banded = banded_of(cells, counts_ref[0, d], wts, d, first_z, band)
        top = grad.astype(jnp.bfloat16)
        rest = (grad - top.astype(jnp.float32)).astype(jnp.bfloat16)
        value = jnp.dot(
            jnp.concatenate([top, rest], axis=0), table_of(cells), preferred_element_type=jnp.float32
        )
        for a in range(3):
            low, high = a * rows_d, (a + 1) * rows_d
            value_a = value[low:high] + value[3 * rows_d + low:3 * rows_d + high]
            out_ref[0, a, pl.ds(d, 1), :] = jnp.sum(value_a * banded, axis=0, keepdims=True)
        return carry

    lax.fori_loop(0, bricks, gather, 0, unroll=2)

    def finish(r, carry):
        for i in range(len(pieces)):
            transfer(i, r).wait_send()
        return carry

    lax.fori_loop(0, n_row, finish, 0)


def body(n_row, n_col, send_cells, send_species, send_mix, send_counts, chi):
    species, domains, slots = send_mix.shape[1:]
    band = NZ // domains
    halves = 2 * n_row
    rows_d = species * band
    pieces = pieces_of(band)
    left, right, along_z = constants_of(species, band)
    rows_h = -(-2 * REACH * species // 8) * 8
    edge_rows = [n_col * n * species for _, _, n, _ in pieces]
    operands = (send_cells, send_species, send_mix, chi, left, right, along_z)
    grid = lambda rows: pltpu.VMEM((halves, n_col, rows, LANES), jnp.float32)
    return pl.pallas_call(
        functools.partial(membrane_kernel, n_row, n_col, band),
        out_shape=jax.ShapeDtypeStruct((1, 3, domains, slots), jnp.float32),
        in_specs=[pl.BlockSpec(memory_space=pltpu.SMEM)] + [pl.BlockSpec(memory_space=pl.ANY)] * 7,
        out_specs=pl.BlockSpec(memory_space=pltpu.VMEM),
        scratch_shapes=[pltpu.VMEM(operand.shape, operand.dtype) for operand in operands]
        + [pltpu.VMEM((n_row, rows, BX * BY), jnp.bfloat16) for rows in edge_rows] * 2
        + [pltpu.VMEM((rows, BX * BY), jnp.float32) for rows in edge_rows]
        + [pltpu.VMEM((species, domains, slots), jnp.float32)]
        + [grid(rows_d), grid(rows_d), grid(rows_h), grid(rows_h), grid(2 * rows_d)]
        + [pltpu.VMEM((4 * rows_d, along_z.shape[2]), jnp.bfloat16)]
        + [
            pltpu.SemaphoreType.DMA((7,)),
            pltpu.SemaphoreType.DMA((len(pieces), n_row)),
            pltpu.SemaphoreType.DMA((len(pieces), n_row)),
        ],
        compiler_params=pltpu.CompilerParams(
            collective_id=0, has_side_effects=True, vmem_limit_bytes=56 * 2**20
        ),
        name="membrane",
    )(send_counts, *operands)


def solution(mesh):
    spec = P(("row", "col"))
    return jax.shard_map(
        functools.partial(body, mesh.shape["row"], mesh.shape["col"]),
        mesh=mesh,
        in_specs=(spec, spec, spec, spec, P()),
        out_specs=spec,
        check_vma=False,
    )
```

time: 74.4 us -> 64.3 us (0.86)
  Pallas kernels: 48.3 us -> 62.5 us
  waiting for transfers between devices: 11.3 us -> 0 us
  starting transfers between devices: 6.49 us -> 0 us
  local copies, waits for them, and re-layouts: 7.73 us -> 1.62 us
    pallas_call x2 -> x1, Pallas kernels: 48.3 us -> 62.5 us  [body(): pl.pallas_call(functools.partial(membrane_kernel, n_row, n_col, band), ou...]
    ppermute x2 -> x0, waiting for transfers between devices: 11.3 us -> none  [body(): lax.ppermute(send, ('row', 'col'), [(i, (i + hop) % domains) for i in ran...]
    ppermute x2 -> x0, starting transfers between devices: 6.49 us -> none  [body(): lax.ppermute(send, ('row', 'col'), [(i, (i + hop) % domains) for i in ran...]
    unnamed x20 -> x1, local copies, waits for them, and re-layouts: 7.73 us -> 1.62 us
  transfers between devices with their start and end apart: 2 -> 0, of which waited for: 2 -> 0; matrix products, arithmetic and copies ran while one was open for 0% -> 0% of each run, Pallas kernels for 0% -> 0%
where the time goes in v2:
time: 64.3 us; the launch traced here: 64.1 us
  Pallas kernels  62.5 us (97%)
  local copies, waits for them, and re-layouts  1.62 us (3%)
    pallas_call x1, Pallas kernels, body(): pl.pallas_call(functools.partial(membrane_kernel, n_row, n_col, band), ou...  62.5 us
    unnamed x1, local copies, waits for them, and re-layouts  1.62 us

profile of v2, /device:TPU:0, one launch (start us, length us, event | category | flops | bytes accessed | tf_op | source)
XLA Modules:
  0.0 64.1 jit_solution(2956043605581759019)
XLA Ops:
  0.0 62.5 %membrane.1 = f32[1,3,32,512]{3,2,1,0:T(8,128)} custom-call(s32[1,32]{1,0:T(1,128)} %counts_ref.1, s32[1,32,512]{2,1,0:T(8,128)} %cells_hbm.1, s32[1,32,512]{2,1,0:T(8,128)} %species_hbm.1, bf16[1,6,32,512]{3,2,1,0:T(8,128)(2,1)} %mix_hbm.1, f32[6,6]{1,0:T(8,128)} %chi_hbm.1, f32[96,6]{1,0:T(8,128)} %constant.6.clone.left_hbm, ...), custom_call_target="tpu_custom_call" | custom-call | tf_op jit(solution)/shard_map/membrane/pallas_call | solution.py:334
  62.5 1.6 %copy.10 = f32[1,3,32,512]{3,2,1,0:T(8,128)} copy(f32[1,3,32,512]{3,2,1,0:T(8,128)} %membrane.1) | data formatting | bytes 393216

commit v3 on v2

--- a/solution.py
+++ b/solution.py
@@ -121,13 +121,23 @@
     return taps[2] * here + taps[3] * one + taps[4] * two
 
 
-def smooth_y(src, dst, h, n_col):
-    for at, size in chunks_of(src.shape[2]):
-        lane_y = lane_y_of(size)
-        rows = [src[h, q, at:at + size] for q in range(n_col)]
-        for q in range(n_col):
-            before, after = roll(rows[q - 1], -BY), roll(rows[(q + 1) % n_col], BY)
-            dst[h, q, at:at + size] = smoothed(moved_y, before, rows[q], after, lane_y)
+def smooth_y(src, r, q):
+    n_col = src.shape[1]
+    out = ([], [])
+    for h in range(2):
+        for at, size in chunks_of(src.shape[2]):
+            lane_y = lane_y_of(size)
+            before = src[2 * r + h, (q + n_col - 1) % n_col, at:at + size]
+            after = src[2 * r + h, (q + 1) % n_col, at:at + size]
+            here = src[2 * r + h, q, at:at + size]
+            out[h].append(smoothed(moved_y, roll(before, -BY), here, roll(after, BY), lane_y))
+    return out
+
+
+def keep(dst, r, q, done):
+    for h in range(2):
+        for (at, size), value in zip(chunks_of(dst.shape[2]), done[h]):
+            dst[2 * r + h, q, at:at + size] = value
 
 
 def smooth_x(src, r, q):
@@ -225,17 +235,16 @@
     maps[:2 * rows_d] = high
     maps[2 * rows_d:] = (full - high.astype(jnp.float32)).astype(jnp.bfloat16)
 
-    def inner_y(h, carry):
-        smooth_y(raw, turned, h, n_col)
-        return carry
-
-    lax.fori_loop(0, halves, inner_y, 0)
+    def inner_y(d, carry):
+        r, q = d // n_col, d % n_col
+        keep(turned, r, q, smooth_y(raw, r, q))
+        return carry
+
+    lax.fori_loop(0, bricks, inner_y, 0, unroll=2)
 
     def inner_x(d, carry):
         r, q = d // n_col, d % n_col
-        for h, done in enumerate(smooth_x(turned, r, q)):
-            for (at, size), value in zip(chunks_of(rows_d), done):
-                raw[2 * r + h, q, at:at + size] = value
+        keep(raw, r, q, smooth_x(turned, r, q))
         return carry
 
     lax.fori_loop(0, bricks, inner_x, 0, unroll=2)
@@ -251,9 +260,12 @@
                 for h in range(2):
                     edge_raw[2 * r + h, q, at:at + rows] = part[q * rows:(q + 1) * rows, h * LANES:(h + 1) * LANES]
                 at += rows
-        for h in range(2):
-            smooth_y(edge_raw, edge_turned, 2 * r + h, n_col)
-        return carry
+
+        def one(q, carry):
+            keep(edge_turned, r, q, smooth_y(edge_raw, r, q))
+            return carry
+
+        return lax.fori_loop(0, n_col, one, carry, unroll=2)
 
     lax.fori_loop(0, n_row, edge_y, 0)
 

time: 64.3 us -> 38.5 us (0.60)
  Pallas kernels: 62.5 us -> 36.7 us
    pallas_call x1, Pallas kernels: 62.5 us -> 36.7 us  [body(): pl.pallas_call(functools.partial(membrane_kernel, n_row, n_col, band), ou...]
where the time goes in v3:
time: 38.5 us; the launch traced here: 38.4 us
  Pallas kernels  36.7 us (95%)
  local copies, waits for them, and re-layouts  1.62 us (4%)
    pallas_call x1, Pallas kernels, body(): pl.pallas_call(functools.partial(membrane_kernel, n_row, n_col, band), ou...  36.7 us
    unnamed x1, local copies, waits for them, and re-layouts  1.62 us

profile of v3, /device:TPU:0, one launch (start us, length us, event | category | flops | bytes accessed | tf_op | source)
XLA Modules:
  0.0 38.4 jit_solution(15281861157261472922)
XLA Ops:
  0.0 36.7 %membrane.1 = f32[1,3,32,512]{3,2,1,0:T(8,128)} custom-call(s32[1,32]{1,0:T(1,128)} %counts_ref.1, s32[1,32,512]{2,1,0:T(8,128)} %cells_hbm.1, s32[1,32,512]{2,1,0:T(8,128)} %species_hbm.1, bf16[1,6,32,512]{3,2,1,0:T(8,128)(2,1)} %mix_hbm.1, f32[6,6]{1,0:T(8,128)} %chi_hbm.1, f32[96,6]{1,0:T(8,128)} %constant.6.clone.left_hbm, ...), custom_call_target="tpu_custom_call" | custom-call | tf_op jit(solution)/shard_map/membrane/pallas_call | solution.py:346
  36.8 1.6 %copy.10 = f32[1,3,32,512]{3,2,1,0:T(8,128)} copy(f32[1,3,32,512]{3,2,1,0:T(8,128)} %membrane.1) | data formatting | bytes 393216

commit v4 on v3

--- a/solution.py
+++ b/solution.py
@@ -77,10 +77,14 @@
     return jnp.concatenate(parts, axis=0)
 
 
-def table_of(cells):
-    plane = lax.shift_right_logical(cells, NZ.bit_length() - 1)
-    ids = lax.broadcasted_iota(jnp.int32, (BX * BY, cells.shape[1]), 0)
-    return jnp.where(plane == ids, 1.0, 0.0).astype(jnp.bfloat16)
+def table_of(cells, ids):
+    plane = lax.shift_right_logical(cells, NZ.bit_length() - 1).astype(jnp.float32).astype(jnp.bfloat16)
+    one, none = jnp.ones((), jnp.bfloat16), jnp.zeros((), jnp.bfloat16)
+    numbers = ids[...]
+    parts = [
+        jnp.where(plane[:, at:at + LANES] == numbers, one, none) for at in range(0, cells.shape[1], LANES)
+    ]
+    return jnp.concatenate(parts, axis=1)
 
 
 def chunks_of(rows):
@@ -159,7 +163,7 @@
     sends, refs = refs[:len(pieces)], refs[len(pieces):]
     recvs, refs = refs[:len(pieces)], refs[len(pieces):]
     stages, refs = refs[:len(pieces)], refs[len(pieces):]
-    wts, raw, turned, edge_raw, edge_turned, fields, maps, load_sem, send_sem, recv_sem = refs
+    wts, raw, turned, edge_raw, edge_turned, fields, maps, ids, load_sem, send_sem, recv_sem = refs
     cells_ref, species_ref, mix_ref, chi_ref, left_ref, right_ref, along_ref = held
     count = wts.shape[0]
     rows_d, rows_h = count * band, edge_raw.shape[2]
@@ -198,6 +202,7 @@
     for load in loads[:3]:
         load.wait()
     fill_weights(species_ref, mix_ref, wts)
+    ids[...] = lax.broadcasted_iota(jnp.int32, ids.shape, 0).astype(jnp.float32).astype(jnp.bfloat16)
     used = 2 * REACH * count
     if rows_h > used:
         edge_raw[:, :, used:] = jnp.zeros((halves, n_col, rows_h - used, LANES), jnp.float32)
@@ -209,7 +214,7 @@
             cells = cells_ref[0, pl.ds(d, 1), :]
             banded = banded_of(cells, counts_ref[0, d], wts, d, first_z, band)
             tile = lax.dot_general(
-                banded.astype(jnp.bfloat16), table_of(cells), (((1,), (1,)), ((), ())),
+                banded.astype(jnp.bfloat16), table_of(cells, ids), (((1,), (1,)), ((), ())),
                 preferred_element_type=jnp.float32,
             )
             raw[2 * r, q] = tile[:, :LANES]
@@ -247,7 +252,7 @@
         keep(raw, r, q, smooth_x(turned, r, q))
         return carry
 
-    lax.fori_loop(0, bricks, inner_x, 0, unroll=2)
+    lax.fori_loop(0, bricks, inner_x, 0, unroll=4)
 
     def edge_y(r, carry):
         for i in range(len(pieces)):
@@ -287,7 +292,7 @@
         fields[2 * r + 1, q] = field[:, LANES:]
         return carry
 
-    lax.fori_loop(0, bricks, to_fields, 0, unroll=2)
+    lax.fori_loop(0, bricks, to_fields, 0, unroll=4)
 
     def gather(d, carry):
         r, q = d // n_col, d % n_col
@@ -314,7 +319,7 @@
         top = grad.astype(jnp.bfloat16)
         rest = (grad - top.astype(jnp.float32)).astype(jnp.bfloat16)
         value = jnp.dot(
-            jnp.concatenate([top, rest], axis=0), table_of(cells), preferred_element_type=jnp.float32
+            jnp.concatenate([top, rest], axis=0), table_of(cells, ids), preferred_element_type=jnp.float32
         )
         for a in range(3):
             low, high = a * rows_d, (a + 1) * rows_d
@@ -322,7 +327,7 @@
             out_ref[0, a, pl.ds(d, 1), :] = jnp.sum(value_a * banded, axis=0, keepdims=True)
         return carry
 
-    lax.fori_loop(0, bricks, gather, 0, unroll=2)
+    lax.fori_loop(0, bricks, gather, 0, unroll=4)
 
     def finish(r, carry):
         for i in range(len(pieces)):
@@ -354,6 +359,7 @@
         + [pltpu.VMEM((species, domains, slots), jnp.float32)]
         + [grid(rows_d), grid(rows_d), grid(rows_h), grid(rows_h), grid(2 * rows_d)]
         + [pltpu.VMEM((4 * rows_d, along_z.shape[2]), jnp.bfloat16)]
+        + [pltpu.VMEM((BX * BY, LANES), jnp.bfloat16)]
         + [
             pltpu.SemaphoreType.DMA((7,)),
             pltpu.SemaphoreType.DMA((len(pieces), n_row)),

time: 38.5 us -> 33.6 us (0.87)
  Pallas kernels: 36.7 us -> 31.8 us
    pallas_call x1, Pallas kernels: 36.7 us -> 31.8 us  [body(): pl.pallas_call(functools.partial(membrane_kernel, n_row, n_col, band), ou...]
where the time goes in v4:
time: 33.6 us; the launch traced here: 33.4 us
  Pallas kernels  31.8 us (95%)
  local copies, waits for them, and re-layouts  1.62 us (5%)
    pallas_call x1, Pallas kernels, body(): pl.pallas_call(functools.partial(membrane_kernel, n_row, n_col, band), ou...  31.8 us
    unnamed x1, local copies, waits for them, and re-layouts  1.62 us

profile of v4, /device:TPU:0, one launch (start us, length us, event | category | flops | bytes accessed | tf_op | source)
XLA Modules:
  0.0 33.4 jit_solution(1583156325135888914)
XLA Ops:
  0.0 31.8 %membrane.1 = f32[1,3,32,512]{3,2,1,0:T(8,128)} custom-call(s32[1,32]{1,0:T(1,128)} %counts_ref.1, s32[1,32,512]{2,1,0:T(8,128)} %cells_hbm.1, s32[1,32,512]{2,1,0:T(8,128)} %species_hbm.1, bf16[1,6,32,512]{3,2,1,0:T(8,128)(2,1)} %mix_hbm.1, f32[6,6]{1,0:T(8,128)} %chi_hbm.1, f32[96,6]{1,0:T(8,128)} %constant.6.clone.left_hbm, ...), custom_call_target="tpu_custom_call" | custom-call | tf_op jit(solution)/shard_map/membrane/pallas_call | solution.py:351
  31.8 1.6 %copy.10 = f32[1,3,32,512]{3,2,1,0:T(8,128)} copy(f32[1,3,32,512]{3,2,1,0:T(8,128)} %membrane.1) | data formatting | bytes 393216

commit v5 on v4

--- a/solution.py
+++ b/solution.py
@@ -292,7 +292,7 @@
         fields[2 * r + 1, q] = field[:, LANES:]
         return carry
 
-    lax.fori_loop(0, bricks, to_fields, 0, unroll=4)
+    lax.fori_loop(0, bricks, to_fields, 0, unroll=8)
 
     def gather(d, carry):
         r, q = d // n_col, d % n_col
@@ -327,7 +327,7 @@
             out_ref[0, a, pl.ds(d, 1), :] = jnp.sum(value_a * banded, axis=0, keepdims=True)
         return carry
 
-    lax.fori_loop(0, bricks, gather, 0, unroll=4)
+    lax.fori_loop(0, bricks, gather, 0, unroll=8)
 
     def finish(r, carry):
         for i in range(len(pieces)):

time: 33.6 us -> 31.3 us (0.932)
  Pallas kernels: 31.8 us -> 29.5 us
    pallas_call x1, Pallas kernels: 31.8 us -> 29.5 us  [body(): pl.pallas_call(functools.partial(membrane_kernel, n_row, n_col, band), ou...]
where the time goes in v5:
time: 31.3 us; the launch traced here: 31.2 us
  Pallas kernels  29.5 us (94%)
  local copies, waits for them, and re-layouts  1.62 us (5%)
    pallas_call x1, Pallas kernels, body(): pl.pallas_call(functools.partial(membrane_kernel, n_row, n_col, band), ou...  29.5 us
    unnamed x1, local copies, waits for them, and re-layouts  1.62 us

profile of v5, /device:TPU:0, one launch (start us, length us, event | category | flops | bytes accessed | tf_op | source)
XLA Modules:
  0.0 31.2 jit_solution(5507044921911560247)
XLA Ops:
  0.0 29.5 %membrane.1 = f32[1,3,32,512]{3,2,1,0:T(8,128)} custom-call(s32[1,32]{1,0:T(1,128)} %counts_ref.1, s32[1,32,512]{2,1,0:T(8,128)} %cells_hbm.1, s32[1,32,512]{2,1,0:T(8,128)} %species_hbm.1, bf16[1,6,32,512]{3,2,1,0:T(8,128)(2,1)} %mix_hbm.1, f32[6,6]{1,0:T(8,128)} %chi_hbm.1, f32[96,6]{1,0:T(8,128)} %constant.6.clone.left_hbm, ...), custom_call_target="tpu_custom_call" | custom-call | tf_op jit(solution)/shard_map/membrane/pallas_call | solution.py:351
  29.5 1.6 %copy.10 = f32[1,3,32,512]{3,2,1,0:T(8,128)} copy(f32[1,3,32,512]{3,2,1,0:T(8,128)} %membrane.1) | data formatting | bytes 393216
